TPU v7x, 768 devices: a whole 4x8x12 slice. The times are simulated.
768 devices in a mesh: blk: 64 (over x, y, z_hi), rep: 12 (over z_lo, core).
Axes of the slice: x: 4, y: 8, z: 12 (z_hi: 2, z_lo: 6; z = z_hi * 6 + z_lo), core: 2. Of those that a mesh axis runs over, the one named last changes fastest.
Arguments:
- features: bfloat16 [786432, 128], P(('blk', 'rep')), may hold values from -6 to 6
- node_scale: float32 [786432], P(('blk', 'rep')), may hold values from 0.02 to 0.2
- weight: bfloat16 [128, 512], replicated, may hold values from -0.5 to 0.5
- bias: float32 [512], replicated, may hold values from -3 to 3
- cotangent: bfloat16 [786432, 512], P(('blk', 'rep')), may hold values from -0.0068359375 to 0.0068359375
- tile_row: int32 [768, 64], P(('blk', 'rep')), may hold values from 0 to 7
- tile_col: int32 [768, 64], P(('blk', 'rep')), may hold values from 0 to 6143, as said below
- edge_weight: bfloat16 [768, 64, 128, 128], P(('blk', 'rep')), may hold values from 0 to 1
- tile_count: int32 [768], P(('blk', 'rep')), may hold values from 1 to 64, as said below
Outputs:
- hidden: bfloat16 [786432, 512], P(('blk', 'rep'))
- grad_weight: float32 [128, 512], replicated
- grad_bias: float32 [512], replicated
Inputs may be any that keep to these rules, and one draw needn't show every extreme that they name: `tile_col`: the column tile of a slot of device d lies in the rows held by loop position d // 12 of blk or by the positions just before or after it on the closed loop of blk. `tile_count`: some device has all 64 slots live.
All inputs are finite; a program needn't handle non-finite values.
Results may differ from a plain program's by a relative error of at most 0.012.
Values may be sent and summed in bfloat16 or wider, within the bound.
A program may use at most 64 MiB of HBM per device.

v0:
```python
import jax
import jax.numpy as jnp
from jax import lax
from jax.sharding import PartitionSpec as P

TILE = 128
BATCH_TILES = 8


def padded(x, sides, width):
    for axis, dim in sides:
        devices, length = (lax.axis_size(axis), x.shape[dim])
        up = [(i, (i + 1) % devices) for i in range(devices)]
        down = [(j, i) for i, j in up]
        last = lax.slice_in_dim(x, length - width, length, axis=dim)
        leading = lax.slice_in_dim(x, 0, width, axis=dim)
        before = lax.ppermute(last, axis, up)
        after = lax.ppermute(leading, axis, down)
        x = jnp.concatenate([before, x, after], axis=dim)
    return x


def shards(
    features, node_scale, weight, bias, cotangent, tile_row, tile_col, edge_weight, tile_count
):
    row_count, feature_width = features.shape
    scaled = (node_scale[:, None] * features.astype(jnp.float32)).astype(jnp.bfloat16)
    group_panel = lax.all_gather(scaled, "rep", axis=0, tiled=True)
    nearby = padded(group_panel, (("blk", 0),), group_panel.shape[0])
    group_tiles = nearby.shape[0] // 3 // TILE
    panel_tiles = nearby.reshape(-1, TILE, feature_width)
    position = lax.axis_index("blk")
    loop_size = lax.axis_size("blk")
    columns = tile_col[0]
    offset = (columns // group_tiles - position) % loop_size
    neighbour = jnp.where(offset == 0, 1, jnp.where(offset == 1, 2, 0))
    source = neighbour * group_tiles + columns % group_tiles
    tile_rows = row_count // TILE
    count_value = tile_count[0]

    def step(block_index, running):
        first_slot = block_index * BATCH_TILES
        picked = lax.dynamic_slice_in_dim(source, first_slot, BATCH_TILES)
        panels = jnp.take(panel_tiles, picked, axis=0)
        tile_values = lax.dynamic_slice_in_dim(edge_weight[0], first_slot, BATCH_TILES)
        slot_ids = first_slot + jnp.arange(BATCH_TILES, dtype=jnp.int32)
        live_flags = (slot_ids < count_value).astype(jnp.bfloat16)
        edge_values = tile_values * live_flags[:, None, None]
        products = jnp.einsum(
            "kij,kjf->kif", edge_values, panels, preferred_element_type=jnp.float32
        )
        targets = lax.dynamic_slice_in_dim(tile_row[0], first_slot, BATCH_TILES)
        onehot = (targets[:, None] == jnp.arange(tile_rows, dtype=jnp.int32)[None, :]).astype(
            jnp.float32
        )
        return running + jnp.einsum("kr,kif->rif", onehot, products)

    start_value = jnp.zeros((tile_rows, TILE, feature_width), jnp.float32)
    running = lax.fori_loop(0, tile_col.shape[1] // BATCH_TILES, step, start_value)
    aggregated = (node_scale[:, None] * running.reshape(row_count, feature_width)).astype(
        jnp.bfloat16
    )
    preact = jnp.dot(aggregated, weight, preferred_element_type=jnp.float32) + bias
    hidden = jnp.where(preact > 0, preact, jnp.expm1(jnp.minimum(preact, 0.0))).astype(jnp.bfloat16)
    derivative = jnp.where(preact > 0, 1.0, jnp.exp(jnp.minimum(preact, 0.0)))
    grad_pre = (cotangent.astype(jnp.float32) * derivative).astype(jnp.bfloat16)
    local_weight = lax.dot_general(
        aggregated, grad_pre, (((0,), (0,)), ((), ())), preferred_element_type=jnp.float32
    )
    local_bias = jnp.sum(grad_pre.astype(jnp.float32), axis=0)
    grad_weight, grad_bias = lax.psum((local_weight, local_bias), ("blk", "rep"))
    return (hidden, grad_weight, grad_bias)


def solution(mesh):
    in_specs = (
        P(("blk", "rep"), None),
        P(("blk", "rep")),
        P(),
        P(),
        P(("blk", "rep"), None),
        P(("blk", "rep"), None),
        P(("blk", "rep"), None),
        P(("blk", "rep"), None, None, None),
        P(("blk", "rep")),
    )
    out_specs = (P(("blk", "rep"), None), P(), P())
    return jax.shard_map(shards, mesh=mesh, in_specs=in_specs, out_specs=out_specs, check_vma=False)
```

profile of v0, /device:TPU:1, one launch (start us, length us, event | category | flops | bytes accessed | tf_op | source)
XLA Modules:
  0.0 1039.1 jit_solution(17266854124967648705)
XLA Ops:
  7.2 1.9 multiply_convert_fusion
  9.2 82.6 %all-gather.2.cloned.1.call-done = bf16[12288,128]{1,0:T(8,128)(2,1)} async-done(((bf16[1024,128]{1,0:T(8,128)(2,1)}), bf16[12288,128]{1,0:T(8,128)(2,1)}) %all-gather.2.cloned.1.call-update) | async-done | bytes 3145744 | tf_op jit(solution)/shard_map/all_gather | solution.py:28
  91.8 5.4 collective-permute-start
  97.2 10.4 collective-permute-start.1
  107.6 0.7 fusion.17
  108.3 330.3 %collective-permute-done = bf16[12288,128]{1,0:T(8,128)(2,1)} collective-permute-done((bf16[12288,128]{1,0:T(8,128)(2,1)}, bf16[12288,128]{1,0:T(8,128)(2,1)}, u32[]{:S(2)}, u32[]{:S(2)}) %collective-permute-start) | collective-permute-done | bytes 3145760 | tf_op jit(solution)/shard_map/ppermute | solution.py:17
  438.6 63.0 %collective-permute-done.1 = bf16[12288,128]{1,0:T(8,128)(2,1)} collective-permute-done((bf16[12288,128]{1,0:T(8,128)(2,1)}, bf16[12288,128]{1,0:T(8,128)(2,1)}, u32[]{:S(2)}, u32[]{:S(2)}) %collective-permute-start.1) | collective-permute-done | bytes 3145760 | tf_op jit(solution)/shard_map/ppermute | solution.py:18
  501.6 13.1 %pad_maximum_fusion = bf16[36864,128]{1,0:T(8,128)(2,1)} fusion(bf16[12288,128]{1,0:T(8,128)(2,1)} %collective-permute-done.1, bf16[12288,128]{1,0:T(8,128)(2,1)} %all-gather.2.cloned.1.call-done, bf16[12288,128]{1,0:T(8,128)(2,1)} %collective-permute-done), kind=kLoop, calls=%fused_computation.20 | loop fusion | flops 28311552 | bytes 18874368 | tf_op jit(solution)/shard_map/concatenate | solution.py:19
  514.7 53.5 %while.14 = (s32[]{:T(128)}, f32[8,128,128]{2,0,1:T(8,128)S(1)}, s32[1,64]{1,0:T(1,128)S(1)}, bf16[1,64,128,128]{3,2,1,0:T(8,128)(2,1)}, s32[]{:T(128)}, /*index...) while((s32[]{:T(128)}, f32[8,128,128]{2,0,1:T(8,128)S(1)}, ...), condition=%wide.region_1.2_spmd.clone, body=%wide.region_0.1_spmd.clone.sunk | while | flops 36177036 | bytes 2625993 | solution.py:59
  514.8 0.8 compare_and_fusion.2
  515.6 4.3 gather_fusion
  519.9 1.2 fusion.33
  521.2 0.3 convolution_add_fusion.2
  521.5 0.7 compare_and_fusion.2
  522.2 4.3 gather_fusion
  526.5 1.3 fusion.33
  527.9 0.3 convolution_add_fusion.2
  528.2 0.7 compare_and_fusion.2
  528.9 4.3 gather_fusion
  533.2 1.2 fusion.33
  534.5 0.3 convolution_add_fusion.2
  534.9 0.7 compare_and_fusion.2
  535.6 4.3 gather_fusion
  539.9 1.2 fusion.33
  541.2 0.3 convolution_add_fusion.2
  541.5 0.7 compare_and_fusion.2
  542.3 4.3 gather_fusion
  546.6 1.2 fusion.33
  547.9 0.3 convolution_add_fusion.2
  548.2 0.7 compare_and_fusion.2
  548.9 4.3 gather_fusion
  553.2 1.2 fusion.33
  554.6 0.3 convolution_add_fusion.2
  554.9 0.7 compare_and_fusion.2
  555.6 4.3 gather_fusion
  559.9 1.2 fusion.33
  561.2 0.3 convolution_add_fusion.2
  561.6 0.7 compare_and_fusion.2
  562.3 4.3 gather_fusion
  566.6 1.2 fusion.33
  567.9 0.3 convolution_add_fusion.2
  568.2 0.1 copy.12
  568.3 0.2 fusion.15
  568.6 2.3 convert_reduce_fusion
  570.9 1.0 fusion.21
  571.9 107.2 %psum.15 = f32[512]{0:T(512)} all-reduce(f32[512]{0:T(512)S(1)} %get-tuple-element.168), channel_id=1, replica_groups=mesh['blk'=64,'rep'=12] {'blk','rep'}, use_global_device_ids=true, to_apply=%region_4.5 | all-reduce | flops 512 | bytes 4096 | tf_op jit(solution)/shard_map/psum | solution.py:71
  679.1 351.4 %all-reduce.2.cloned.1.call-done = f32[128,512]{1,0:T(8,128)} async-done(((f32[128,512]{1,0:T(8,128)}), f32[128,512]{1,0:T(8,128)}) %all-reduce.2.cloned.1.call-update) | async-done | bytes 262160 | tf_op jit(solution)/shard_map/psum | solution.py:71
  1030.5 1.7 copy.25
  (31 shorter events, 0.8 us)
Async XLA Ops:
  7.2 561.4 %copy-start = (bf16[128,512]{1,0:T(8,128)(2,1)S(1)}, bf16[128,512]{1,0:T(8,128)(2,1)}, u32[]{:S(2)}) copy-start(bf16[128,512]{1,0:T(8,128)(2,1)} %param.13) | copy-start | bytes 393220
  7.2 84.6 %all-gather.2.cloned.1.call-start = ((), (), s32[]{:S(2)}) async-start(), calls=%async_computation | async-start | bytes 3407872 | tf_op jit(solution)/shard_map/all_gather | solution.py:28
  9.1 1021.4 %all-reduce.2.cloned.1.call-start = ((), (), s32[]{:S(2)}) async-start(), calls=%async_computation.1 | async-start | bytes 524288 | tf_op jit(solution)/shard_map/psum | solution.py:71
  91.8 346.8 %collective-permute-start = (bf16[12288,128]{1,0:T(8,128)(2,1)}, bf16[12288,128]{1,0:T(8,128)(2,1)}, u32[]{:S(2)}, u32[]{:S(2)}) collective-permute-start(bf16[12288,128]{1,0:T(8,128)(2,1)} %all-gather.2.cloned.1.call-done), channel_id=1, source_target_pairs={{0,12},{12,24},{24,36},{36,48},{48,60},{60,72},{72,84},{84,96},{96... | collective-permute-start | bytes 9437192 | tf_op jit(solution)/shard_map/ppermute | solution.py:17
  97.2 404.3 %collective-permute-start.1 = (bf16[12288,128]{1,0:T(8,128)(2,1)}, bf16[12288,128]{1,0:T(8,128)(2,1)}, u32[]{:S(2)}, u32[]{:S(2)}) collective-permute-start(bf16[12288,128]{1,0:T(8,128)(2,1)} %all-gather.2.cloned.1.call-done), channel_id=1, source_target_pairs={{12,0},{24,12},{36,24},{48,36},{60,48},{72,60},{84,72},{96,84},{10... | collective-permute-start | bytes 9437192 | tf_op jit(solution)/shard_map/ppermute | solution.py:18
  108.3 406.4 %copy-start.4 = (s32[1,64]{1,0:T(1,128)S(1)}, s32[1,64]{1,0:T(1,128)}, u32[]{:S(2)}) copy-start(s32[1,64]{1,0:T(1,128)} %param.16) | copy-start | bytes 772
  514.7 53.6 %copy-start.1 = (f32[1024]{0:T(1024)S(1)}, f32[1024]{0:T(1024)}, u32[]{:S(2)}) copy-start(f32[1024]{0:T(1024)} %param.12) | copy-start | bytes 12292
  514.7 53.8 %copy-start.2 = (bf16[1024,512]{1,0:T(8,128)(2,1)S(1)}, bf16[1024,512]{1,0:T(8,128)(2,1)}, u32[]{:S(2)}) copy-start(bf16[1024,512]{1,0:T(8,128)(2,1)} %param.15) | copy-start | bytes 3145732
  514.7 53.8 %copy-start.3 = (f32[512]{0:T(512)S(1)}, f32[512]{0:T(512)}, u32[]{:S(2)}) copy-start(f32[512]{0:T(512)} %param.14) | copy-start | bytes 6148
Sparse Core Ops, SparseCore 0:
  11.0 80.7 all-gather.1
  572.0 458.4 all-reduce.1
where the time goes:
time: 1040 us
  waiting for transfers between devices  827 us (80%)
  blocking collectives  107 us (10%)
  local copies, waits for them, and re-layouts  36.6 us (4%)
  other arithmetic  21.8 us (2%)
  starting transfers between devices  15.9 us (2%)
  matrix products  15.6 us (2%)
  between operations  14.2 us (1%)
    psum x1, waiting for transfers between devices, shards(): lax.psum((local_weight, local_bias), ('blk', 'rep'))  351 us
    ppermute x1, waiting for transfers between devices, padded(): before = lax.ppermute(last, axis, up)  330 us
    psum x1, blocking collectives, shards(): lax.psum((local_weight, local_bias), ('blk', 'rep'))  107 us
    all_gather x1, waiting for transfers between devices, shards(): group_panel = lax.all_gather(scaled, 'rep', axis=0, tiled=True)  82.6 us
    ppermute x1, waiting for transfers between devices, padded(): after = lax.ppermute(leading, axis, down)  63 us
    gather x8, local copies, waits for them, and re-layouts, step(): panels = jnp.take(panel_tiles, picked, axis=0)  34.2 us
  transfers between devices with their start and end apart: 4, of which 4 were waited for; matrix products, arithmetic and copies ran while one was open for 0% of the time, Pallas kernels for 0%

commit v1 on v0

v1 whole, which is shorter than its diff:
```python
import functools

import jax
import jax.numpy as jnp
from jax import lax
from jax.experimental import pallas as pl
from jax.experimental.pallas import tpu as pltpu
from jax.sharding import PartitionSpec as P

TILE = 128
BATCH = 8
PARTS = 4
SKEW = 2
LAG = 3
MESH = pl.DeviceIdType.MESH
VMEM_LIMIT = 48 * 1024 * 1024


def spread(row):
    return jnp.transpose(jnp.broadcast_to(row, (TILE, TILE)))


def place(columns, half):
    blk, rep = lax.axis_index("blk"), lax.axis_index("rep")
    upper = lax.rem(blk, 2)
    core = lax.rem(rep, 2)
    chip = upper * half + lax.div(rep, 2)
    return blk, rep, lax.div(blk, 2), upper, chip, core


def greet(partners):
    barrier = pltpu.get_barrier_semaphore()
    for partner in partners:
        pl.semaphore_signal(barrier, inc=1, device_id=partner, device_id_type=MESH)
    pl.semaphore_wait(barrier, len(partners))


def gather_kernel(
    columns, half, features, scale, out, mine, ring_recv, side_recv, mate_recv, ring_sent, side_sent, mate_sent, kept
):
    chips = 2 * half
    rows = features.shape[0]
    part = rows // PARTS
    blk, rep, column, upper, chip, core = place(columns, half)
    way = 1 - 2 * core

    def chip_id(c):
        return (2 * column + lax.div(c, half), 2 * lax.rem(c, half) + core)

    def around(steps):
        return lax.rem(chip + way * steps + 2 * chips, chips)

    ahead, behind = chip_id(around(1)), chip_id(around(-1))
    turn = 1 - 2 * upper
    side_to = (2 * lax.rem(column + turn + columns, columns) + upper, rep)
    side_from = (2 * lax.rem(column - turn + columns, columns) + upper, rep)
    mate = (blk, rep + way)
    greet((ahead, behind, side_to, side_from, mate))

    for t in range(rows // TILE):
        span = pl.ds(t * TILE, TILE)
        mine[span, :] = (spread(scale[pl.ds(t, 1), :]) * features[span, :].astype(jnp.float32)).astype(mine.dtype)
    own = 2 * chip + core
    keep = pltpu.make_async_copy(mine, out.at[own], kept)
    keep.start()

    def chunk(q):
        return pl.ds(pl.multiple_of(q * part, part), part)

    def ring(direction, step, q, source, piece, target):
        return pltpu.make_async_remote_copy(
            src_ref=source,
            dst_ref=out.at[piece, chunk(q)],
            send_sem=ring_sent,
            recv_sem=ring_recv.at[(direction * half + step) * PARTS + q],
            device_id=target,
            device_id_type=MESH,
        )

    def side(direction, step, q, piece):
        return pltpu.make_async_remote_copy(
            src_ref=out.at[piece, chunk(q)],
            dst_ref=out.at[2 * chips + lax.rem(piece, 2 * half), chunk(q)],
            send_sem=side_sent,
            recv_sem=side_recv.at[(direction * half + step) * PARTS + q],
            device_id=side_to,
            device_id_type=MESH,
        )

    def share(source, piece, q):
        pltpu.make_async_remote_copy(
            src_ref=source,
            dst_ref=out.at[piece, chunk(q)],
            send_sem=mate_sent,
            recv_sem=mate_recv,
            device_id=mate,
            device_id_type=MESH,
        ).start()

    lengths = (half, half - 1)
    targets = (ahead, behind)

    def arrived(direction, step):
        c = around(-step if direction == 0 else step)
        return 2 * c + core, lax.div(c, half) != upper

    def tick(time, _):
        def each(q, _):
            step = time - SKEW * q

            @pl.when(step == 0)
            def _():
                source = mine.at[chunk(q)]
                ring(0, 0, q, source, own, ahead).start()
                ring(1, 0, q, source, own, behind).start()
                share(source, own, q)

            for direction in range(2):

                @pl.when((step >= 1) & (step <= lengths[direction]))
                def _():
                    piece, foreign = arrived(direction, step)
                    here = out.at[piece, chunk(q)]
                    ring(direction, step - 1, q, here, piece, targets[direction]).wait_recv()

                    @pl.when(step < lengths[direction])
                    def _():
                        ring(direction, step, q, here, piece, targets[direction]).start()

                    @pl.when(foreign)
                    def _():
                        side(direction, step - 1, q, piece).start()

                    share(here, piece, q)

            late = step - LAG
            for direction in range(2):

                @pl.when((late >= 1) & (late <= lengths[direction]))
                def _():
                    piece, foreign = arrived(direction, late)

                    @pl.when(foreign)
                    def _():
                        side(direction, late - 1, q, piece).wait_recv()
                        third = 2 * chips + lax.rem(piece, 2 * half)
                        share(out.at[third, chunk(q)], third, q)

            return 0

        return lax.fori_loop(0, PARTS, each, 0)

    lax.fori_loop(0, half + SKEW * (PARTS - 1) + LAG + 1, tick, 0)

    def drain(pieces, semaphore):
        span = out.at[pl.ds(0, pieces)]
        pltpu.make_async_copy(span, span, semaphore).wait()

    keep.wait()
    drain(chips - 1, ring_sent)
    drain(half, side_sent)
    drain(chips + half, mate_sent)
    drain(chips + half, mate_recv)


def layer_kernel(
    half, tile_row, tile_col, tile_count, panels, edges, scale, weight, bias, cotangent, hidden, grad, grad_bias,
    picked, values, upstream, total, slot_sem, value_sem, up_sem,
):
    slots = edges.shape[0]
    rows = total.shape[0]
    width = weight.shape[1]
    blk = lax.axis_index("blk")
    blks = lax.axis_size("blk")
    upper = lax.rem(blk, 2)
    live = tile_count[0]
    batches = lax.div(live + (BATCH - 1), BATCH)
    tiles = rows // TILE
    group_tiles = 2 * half * tiles

    cotangent_copy = pltpu.make_async_copy(cotangent, upstream, up_sem)

    def values_copy(b):
        span = pl.ds(b * BATCH, BATCH)
        return pltpu.make_async_copy(edges.at[span], values.at[span], value_sem.at[b])

    def fetch(b, _):
        values_copy(b).start()
        for i in range(BATCH):
            k = b * BATCH + i
            col = tile_col[0, k]
            position = lax.div(col, group_tiles)
            offset = lax.rem(position - blk + blks, blks)
            part = jnp.where(offset == 0, upper, jnp.where(offset == jnp.where(upper == 0, 1, blks - 1), 1 - upper, 2))
            tile = part * group_tiles + lax.rem(col, group_tiles)
            pltpu.make_async_copy(panels.at[tile], picked.at[k], slot_sem.at[b]).start()
        return 0

    lax.fori_loop(0, batches, fetch, 0)
    cotangent_copy.start()
    total[...] = jnp.zeros_like(total)

    def multiply(b, _):
        values_copy(b).wait()
        span = pl.ds(b * BATCH, BATCH)
        pltpu.make_async_copy(picked.at[span], picked.at[span], slot_sem.at[b]).wait()
        products = []
        for i in range(BATCH):
            k = b * BATCH + i
            product = jnp.dot(values[k], picked[k], preferred_element_type=jnp.float32)
            products.append(jnp.where(k < live, product, 0.0))
        for i in range(BATCH):
            start = pl.multiple_of(tile_row[0, b * BATCH + i] * TILE, TILE)
            total[pl.ds(start, TILE), :] += products[i]
        return 0

    lax.fori_loop(0, batches, multiply, 0)
    cotangent_copy.wait()
    grad_total = jnp.zeros((TILE, width), jnp.float32)
    bias_total = jnp.zeros((8, width), jnp.float32)
    for t in range(tiles):
        span = pl.ds(t * TILE, TILE)
        aggregated = (spread(scale[pl.ds(t, 1), :]) * total[span, :]).astype(jnp.bfloat16)
        preact = jnp.dot(aggregated, weight[...], preferred_element_type=jnp.float32) + bias[...]
        positive = preact > 0
        power = jnp.exp(jnp.minimum(preact, 0.0))
        hidden[span, :] = jnp.where(positive, preact, power - 1.0).astype(hidden.dtype)
        grad_pre = (upstream[span, :].astype(jnp.float32) * jnp.where(positive, 1.0, power)).astype(jnp.bfloat16)
        grad_total += lax.dot_general(
            aggregated, grad_pre, (((0,), (0,)), ((), ())), preferred_element_type=jnp.float32
        )
        bias_total += jnp.sum(grad_pre.astype(jnp.float32).reshape(TILE // 8, 8, width), axis=0)
    lanes = width // TILE
    for i in range(TILE // 8):
        for j in range(lanes):
            grad[i * lanes + j] = grad_total[8 * i : 8 * i + 8, TILE * j : TILE * (j + 1)]
    bias_row = jnp.sum(bias_total, axis=0, keepdims=True)
    grad_bias[...] = jnp.zeros_like(grad_bias)
    for j in range(lanes):
        grad_bias[j : j + 1, :] = bias_row[:, TILE * j : TILE * (j + 1)]


def sum_kernel(
    columns, half, grad, grad_bias, out, out_bias,
    from_mate, bias_mate, message, inbox, line, full,
    mate_recv, bias_recv, plane_recv, line_recv, back_recv, last_recv,
    mate_sent, bias_sent, plane_sent, line_sent, back_sent, last_sent,
):
    chips = 2 * half
    blk, rep, column, upper, chip, core = place(columns, half)
    share = grad.shape[0] // 2 // columns
    mate = (blk, rep + 1 - 2 * core)

    def plane_id(j):
        return (2 * j + upper, rep)

    def line_id(c):
        return (2 * column + lax.div(c, half), 2 * lax.rem(c, half) + core)

    barrier = pltpu.get_barrier_semaphore()

    def greet_plane(o, _):
        pl.semaphore_signal(barrier, inc=1, device_id=plane_id(lax.rem(column + o, columns)), device_id_type=MESH)
        return 0

    def greet_line(o, _):
        pl.semaphore_signal(barrier, inc=1, device_id=line_id(lax.rem(chip + o, chips)), device_id_type=MESH)
        return 0

    pl.semaphore_signal(barrier, inc=1, device_id=mate, device_id_type=MESH)
    lax.fori_loop(1, columns, greet_plane, 0)
    lax.fori_loop(1, chips, greet_line, 0)
    pl.semaphore_wait(barrier, columns + chips - 1)

    count = columns * share

    def remote(source, target, sent, received, device):
        return pltpu.make_async_remote_copy(
            src_ref=source, dst_ref=target, send_sem=sent, recv_sem=received, device_id=device, device_id_type=MESH
        )

    other = remote(grad.at[pl.ds((1 - core) * count, count)], from_mate, mate_sent, mate_recv, mate)
    other.start()
    other_bias = remote(grad_bias, bias_mate, bias_sent, bias_recv, mate)
    other_bias.start()
    other_bias.wait()
    bias_sum = grad_bias[...] + bias_mate[...]
    other.wait()
    for j in range(columns):
        for i in range(share):
            message[j, 8 * i : 8 * i + 8, :] = grad[core * count + j * share + i] + from_mate[j * share + i]
        message[j, 8 * share :, :] = bias_sum

    def send_plane(o, _):
        j = lax.rem(column + o, columns)
        remote(message.at[j], inbox.at[column], plane_sent, plane_recv, plane_id(j)).start()
        return 0

    lax.fori_loop(1, columns, send_plane, 0)
    inbox[column] = message[column]
    pltpu.make_async_copy(inbox.at[pl.ds(1, columns - 1)], inbox.at[pl.ds(1, columns - 1)], plane_recv).wait()
    line[chip] = jnp.sum(inbox[...], axis=0)

    def send_line(o, _):
        c = lax.rem(chip + o, chips)
        remote(line.at[chip], line.at[chip], line_sent, line_recv, line_id(c)).start()
        return 0

    lax.fori_loop(1, chips, send_line, 0)
    pltpu.make_async_copy(line.at[pl.ds(1, chips - 1)], line.at[pl.ds(1, chips - 1)], line_recv).wait()
    final = jnp.sum(line[...], axis=0)
    base = core * columns + column
    for i in range(share):
        full[base, i] = final[8 * i : 8 * i + 8, :]
    out_bias[...] = final[8 * share :, :]

    def send_back(o, _):
        j = lax.rem(column + o, columns)
        remote(full.at[base], full.at[base], back_sent, back_recv, plane_id(j)).start()
        return 0

    lax.fori_loop(1, columns, send_back, 0)
    pltpu.make_async_copy(full.at[pl.ds(1, columns - 1)], full.at[pl.ds(1, columns - 1)], back_recv).wait()
    mine = full.at[pl.ds(core * columns, columns)]
    last = remote(mine, mine, last_sent, last_recv, mate)
    last.start()
    last.wait()
    lanes = out.shape[1] // TILE
    for j in range(2 * columns):
        for i in range(share):
            n = j * share + i
            r, c = divmod(n, lanes)
            out[8 * r : 8 * r + 8, TILE * c : TILE * (c + 1)] = full[j, i]
    pltpu.make_async_copy(message.at[pl.ds(1, columns - 1)], message.at[pl.ds(1, columns - 1)], plane_sent).wait()
    pltpu.make_async_copy(line.at[pl.ds(1, chips - 1)], line.at[pl.ds(1, chips - 1)], line_sent).wait()
    pltpu.make_async_copy(full.at[pl.ds(1, columns - 1)], full.at[pl.ds(1, columns - 1)], back_sent).wait()


def shards(features, node_scale, weight, bias, cotangent, tile_row, tile_col, edge_weight, tile_count):
    rows, depth = features.shape
    width = weight.shape[1]
    slots = tile_col.shape[1]
    columns = lax.axis_size("blk") // 2
    half = lax.axis_size("rep") // 2
    chips = 2 * half
    pieces = 2 * chips + 2 * half
    scale = node_scale.reshape(rows // TILE, TILE)
    vmem = pl.BlockSpec(memory_space=pltpu.VMEM)
    smem = pl.BlockSpec(memory_space=pltpu.SMEM)
    hbm = pl.BlockSpec(memory_space=pl.ANY)
    dma = pltpu.SemaphoreType.DMA

    gathered = pl.pallas_call(
        functools.partial(gather_kernel, columns, half),
        name="gather",
        out_shape=jax.ShapeDtypeStruct((pieces, rows, depth), jnp.bfloat16),
        in_specs=[vmem, vmem],
        out_specs=hbm,
        scratch_shapes=[
            pltpu.VMEM((rows, depth), jnp.bfloat16),
            dma((2 * half * PARTS,)),
            dma((2 * half * PARTS,)),
            dma(()),
            dma(()),
            dma(()),
            dma(()),
            dma(()),
        ],
        compiler_params=pltpu.CompilerParams(
            collective_id=0, has_side_effects=True, vmem_limit_bytes=VMEM_LIMIT
        ),
    )(features, scale)

    chunks = TILE * width // (8 * TILE)
    hidden, grad, grad_bias = pl.pallas_call(
        functools.partial(layer_kernel, half),
        name="layer",
        out_shape=(
            jax.ShapeDtypeStruct((rows, width), jnp.bfloat16),
            jax.ShapeDtypeStruct((chunks, 8, TILE), jnp.float32),
            jax.ShapeDtypeStruct((8, TILE), jnp.float32),
        ),
        in_specs=[smem, smem, smem, hbm, hbm, vmem, vmem, vmem, hbm],
        out_specs=(vmem, vmem, vmem),
        scratch_shapes=[
            pltpu.VMEM((slots, TILE, depth), jnp.bfloat16),
            pltpu.VMEM((slots, TILE, TILE), jnp.bfloat16),
            pltpu.VMEM((rows, width), jnp.bfloat16),
            pltpu.VMEM((rows, depth), jnp.float32),
            dma((slots // BATCH,)),
            dma((slots // BATCH,)),
            dma(()),
        ],
        compiler_params=pltpu.CompilerParams(vmem_limit_bytes=VMEM_LIMIT),
    )(
        tile_row, tile_col, tile_count, gathered.reshape(-1, TILE, depth), edge_weight[0], scale, weight,
        bias.reshape(1, width), cotangent,
    )

    share = chunks // 2 // columns
    tall = 8 * share + 8
    grad_weight, bias_sum = pl.pallas_call(
        functools.partial(sum_kernel, columns, half),
        name="sum",
        out_shape=(
            jax.ShapeDtypeStruct((TILE, width), jnp.float32),
            jax.ShapeDtypeStruct((8, TILE), jnp.float32),
        ),
        in_specs=[vmem, vmem],
        out_specs=(vmem, vmem),
        scratch_shapes=[
            pltpu.VMEM((chunks // 2, 8, TILE), jnp.float32),
            pltpu.VMEM((8, TILE), jnp.float32),
            pltpu.VMEM((columns, tall, TILE), jnp.float32),
            pltpu.VMEM((columns, tall, TILE), jnp.float32),
            pltpu.VMEM((chips, tall, TILE), jnp.float32),
            pltpu.VMEM((2 * columns, share, 8, TILE), jnp.float32),
        ]
        + [dma(())] * 12,
        compiler_params=pltpu.CompilerParams(
            collective_id=1, has_side_effects=True, vmem_limit_bytes=VMEM_LIMIT
        ),
    )(grad, grad_bias)
    return hidden, grad_weight, bias_sum.reshape(-1)[:width]


def solution(mesh):
    rows = P(("blk", "rep"))
    in_specs = (
        P(("blk", "rep"), None),
        rows,
        P(),
        P(),
        P(("blk", "rep"), None),
        P(("blk", "rep"), None),
        P(("blk", "rep"), None),
        P(("blk", "rep"), None, None, None),
        rows,
    )
    out_specs = (P(("blk", "rep"), None), P(), P())
    return jax.shard_map(shards, mesh=mesh, in_specs=in_specs, out_specs=out_specs, check_vma=False)
```

time: 1040 us -> 119 us (0.11)
  waiting for transfers between devices: 827 us -> 0 us
  Pallas kernels: 0 us -> 115 us
  blocking collectives: 107 us -> 0 us
  local copies, waits for them, and re-layouts: 36.6 us -> 3.08 us
  other arithmetic: 21.8 us -> 0 us
  starting transfers between devices: 15.9 us -> 0 us
  matrix products: 15.6 us -> 0 us
  between operations: 14.2 us -> 1.53 us
    ppermute x2 -> x0, waiting for transfers between devices: 393 us -> none  [the longest x1 330 us: padded(): before = lax.ppermute(last, axis, up)]
    psum x1 -> x0, waiting for transfers between devices: 351 us -> none  [shards(): lax.psum((local_weight, local_bias), ('blk', 'rep'))]
    pallas_call x0 -> x3, Pallas kernels: none -> 115 us  [the longest x1 76.4 us: shards(): pl.pallas_call(functools.partial(gather_kernel, columns, half), name='gat...]
    psum x1 -> x0, blocking collectives: 107 us -> none  [shards(): lax.psum((local_weight, local_bias), ('blk', 'rep'))]
    all_gather x1 -> x0, waiting for transfers between devices: 82.6 us -> none  [shards(): group_panel = lax.all_gather(scaled, 'rep', axis=0, tiled=True)]
    gather x8 -> x0, local copies, waits for them, and re-layouts: 34.2 us -> none  [step(): panels = jnp.take(panel_tiles, picked, axis=0)]
    ppermute x2 -> x0, starting transfers between devices: 15.8 us -> none  [the longest x1 10.4 us: padded(): after = lax.ppermute(leading, axis, down)]
    dot_general x18 -> x0, matrix products: 15.6 us -> none  [the longest x8 10 us: step(): jnp.einsum('kij,kjf->kif', edge_values, panels, preferred_element_type=jn...]
  transfers between devices with their start and end apart: 4 -> 0, of which waited for: 4 -> 0; matrix products, arithmetic and copies ran while one was open for 0% -> 0% of each run, Pallas kernels for 0% -> 0%
where the time goes in v1:
time: 119 us
  Pallas kernels  115 us (97%)
  local copies, waits for them, and re-layouts  3.08 us (3%)
  between operations  1.53 us (1%)
    pallas_call x1, Pallas kernels, shards(): pl.pallas_call(functools.partial(gather_kernel, columns, half), name='gat...  76.4 us
    pallas_call x1, Pallas kernels, shards(): pl.pallas_call(functools.partial(sum_kernel, columns, half), name='sum',...  32.5 us
    pallas_call x1, Pallas kernels, shards(): pl.pallas_call(functools.partial(layer_kernel, half), name='layer', out_s...  5.66 us
    unnamed x17, local copies, waits for them, and re-layouts  2.5 us

profile of v1, /device:TPU:1, one launch (start us, length us, event | category | flops | bytes accessed | tf_op | source)
XLA Modules:
  0.0 119.2 jit_solution(5323619951865598967)
XLA Ops:
  0.6 0.0 copy-start
  0.6 0.0 copy-start.1
  1.4 0.0 copy-start.2
  1.5 1.1 copy-done.2
  2.5 0.0 copy-start.4
  2.5 0.7 copy-done.4
  3.2 0.0 copy-start.3
  3.2 0.0 copy-start.5
  3.2 0.0 copy-start.6
  3.2 0.0 copy-start.7
  3.2 76.4 %gather.1 = bf16[36,1024,128]{2,1,0:T(8,128)(2,1)} custom-call(bf16[1024,128]{1,0:T(8,128)(2,1)S(1)} %copy-done.2, f32[8,128]{1,0:T(8,128)S(1)} %bitcast.7), custom_call_target="tpu_custom_call" | custom-call | tf_op jit(solution)/shard_map/gather/pallas_call | solution.py:353
  79.7 0.0 copy-done
  79.7 0.0 copy-done.1
  79.7 0.0 copy-done.3
  79.7 0.0 copy-done.5
  79.7 0.0 copy-done.6
  79.7 0.0 copy-done.7
  79.7 5.7 %layer.1 = (bf16[1024,512]{1,0:T(8,128)(2,1)}, f32[64,8,128]{2,1,0:T(8,128)S(1)}, f32[8,128]{1,0:T(8,128)S(1)}) custom-call(s32[1,64]{1,0:T(1,128)S(1)} %copy-done.6, s32[1,64]{1,0:T(1,128)S(1)} %copy-done.7, s32[1]{0:T(128)S(6)} %copy.13.tile_count, bf16[288,128,128]{2,1,0:T(8,128)(2,1)} %bitcast.10, bf16[64,128,128]{2,1,0:T(8,128)(2,1)S(1)} %bitcast.6, ...), custom_call_target="tpu_custom_call" | custom-call | tf_op jit(solution)/shard_map/layer/pallas_call | solution.py:375
  85.4 32.5 %sum.1 = (f32[128,512]{1,0:T(8,128)S(1)}, f32[8,128]{1,0:T(8,128)S(1)}) custom-call(f32[64,8,128]{2,1,0:T(8,128)S(1)} %get-tuple-element.9.grad, f32[8,128]{1,0:T(8,128)S(1)} %get-tuple-element.10.grad_bias), custom_call_target="tpu_custom_call" | custom-call | tf_op jit(solution)/shard_map/sum/pallas_call | solution.py:402
  117.9 0.6 slice_bitcast_fusion
  118.5 0.7 copy.14
Async XLA Ops:
  0.6 79.0 %copy-start = (bf16[1,64,128,128]{3,2,1,0:T(8,128)(2,1)S(1)}, bf16[1,64,128,128]{3,2,1,0:T(8,128)(2,1)}, u32[]{:S(2)}) copy-start(bf16[1,64,128,128]{3,2,1,0:T(8,128)(2,1)} %param.16) | copy-start | bytes 6291460
  0.6 79.0 %copy-start.1 = (bf16[1024,512]{1,0:T(8,128)(2,1)S(1)}, bf16[1024,512]{1,0:T(8,128)(2,1)}, u32[]{:S(2)}) copy-start(bf16[1024,512]{1,0:T(8,128)(2,1)} %cotangent.1) | copy-start | bytes 3145732
  1.4 1.1 copy-start.2
  2.5 0.7 copy-start.4
  3.2 76.4 %copy-start.3 = (bf16[128,512]{1,0:T(8,128)(2,1)S(1)}, bf16[128,512]{1,0:T(8,128)(2,1)}, u32[]{:S(2)}) copy-start(bf16[128,512]{1,0:T(8,128)(2,1)} %weight.1) | copy-start | bytes 393220
  3.2 76.4 %copy-start.5 = (f32[512]{0:T(512)S(1)}, f32[512]{0:T(512)}, u32[]{:S(2)}) copy-start(f32[512]{0:T(512)} %param.12) | copy-start | bytes 6148
  3.2 76.5 %copy-start.6 = (s32[1,64]{1,0:T(1,128)S(1)}, s32[1,64]{1,0:T(1,128)}, u32[]{:S(2)}) copy-start(s32[1,64]{1,0:T(1,128)} %tile_row.1) | copy-start | bytes 772
  3.2 76.5 %copy-start.7 = (s32[1,64]{1,0:T(1,128)S(1)}, s32[1,64]{1,0:T(1,128)}, u32[]{:S(2)}) copy-start(s32[1,64]{1,0:T(1,128)} %tile_col.1) | copy-start | bytes 772

commit v2 on v1

v2 whole, which is shorter than its diff:
```python
import functools

import jax
import jax.numpy as jnp
from jax import lax
from jax.experimental import pallas as pl
from jax.experimental.pallas import tpu as pltpu
from jax.sharding import PartitionSpec as P

TILE = 128
BATCH = 8
PARTS = 4
SKEW = 0
LAG = 3
WIRE = jnp.bfloat16
ACROSS = 8
MESH = pl.DeviceIdType.MESH
VMEM_LIMIT = 24 * 1024 * 1024


def spread(row):
    return jnp.transpose(jnp.broadcast_to(row, (TILE, TILE)))


def place(columns, half):
    blk, rep = lax.axis_index("blk"), lax.axis_index("rep")
    upper = lax.rem(blk, 2)
    core = lax.rem(rep, 2)
    chip = upper * half + lax.div(rep, 2)
    return blk, rep, lax.div(blk, 2), upper, chip, core


def gather_kernel(
    columns, half, features, scale, out, mine, ring_recv, side_recv, mate_recv, ring_sent, side_sent, mate_sent, kept
):
    chips = 2 * half
    rows = features.shape[0]
    part = rows // PARTS
    blk, rep, column, upper, chip, core = place(columns, half)
    way = 1 - 2 * core

    def chip_id(c):
        return (2 * column + lax.div(c, half), 2 * lax.rem(c, half) + core)

    def around(steps):
        return lax.rem(chip + way * steps + 2 * chips, chips)

    ahead, behind = chip_id(around(1)), chip_id(around(-1))
    turn = 1 - 2 * upper
    side_to = (2 * lax.rem(column + turn + columns, columns) + upper, rep)
    side_from = (2 * lax.rem(column - turn + columns, columns) + upper, rep)
    mate = (blk, rep + way)
    partners = (ahead, behind, side_to, side_from, mate)
    barrier = pltpu.get_barrier_semaphore()
    for partner in partners:
        pl.semaphore_signal(barrier, inc=1, device_id=partner, device_id_type=MESH)

    for t in range(rows // TILE):
        span = pl.ds(t * TILE, TILE)
        mine[span, :] = (spread(scale[pl.ds(t, 1), :]) * features[span, :].astype(jnp.float32)).astype(mine.dtype)
    pl.semaphore_wait(barrier, len(partners))
    own = 2 * chip + core
    keep = pltpu.make_async_copy(mine, out.at[own], kept)
    keep.start()

    def chunk(q):
        return pl.ds(pl.multiple_of(q * part, part), part)

    def ring(direction, step, q, source, piece, target):
        return pltpu.make_async_remote_copy(
            src_ref=source,
            dst_ref=out.at[piece, chunk(q)],
            send_sem=ring_sent,
            recv_sem=ring_recv.at[(direction * half + step) * PARTS + q],
            device_id=target,
            device_id_type=MESH,
        )

    def side(direction, step, q, piece):
        return pltpu.make_async_remote_copy(
            src_ref=out.at[piece, chunk(q)],
            dst_ref=out.at[2 * chips + lax.rem(piece, 2 * half), chunk(q)],
            send_sem=side_sent,
            recv_sem=side_recv.at[(direction * half + step) * PARTS + q],
            device_id=side_to,
            device_id_type=MESH,
        )

    def share(source, piece, q):
        pltpu.make_async_remote_copy(
            src_ref=source,
            dst_ref=out.at[piece, chunk(q)],
            send_sem=mate_sent,
            recv_sem=mate_recv,
            device_id=mate,
            device_id_type=MESH,
        ).start()

    lengths = (half, half - 1)
    targets = (ahead, behind)

    def arrived(direction, step):
        c = around(-step if direction == 0 else step)
        return 2 * c + core, lax.div(c, half) != upper

    def tick(time, _):
        def each(q, _):
            step = time - SKEW * q

            @pl.when(step == 0)
            def _():
                source = mine.at[chunk(q)]
                ring(0, 0, q, source, own, ahead).start()
                ring(1, 0, q, source, own, behind).start()
                share(source, own, q)

            for direction in range(2):

                @pl.when((step >= 1) & (step <= lengths[direction]))
                def _():
                    piece, foreign = arrived(direction, step)
                    here = out.at[piece, chunk(q)]
                    ring(direction, step - 1, q, here, piece, targets[direction]).wait_recv()

                    @pl.when(step < lengths[direction])
                    def _():
                        ring(direction, step, q, here, piece, targets[direction]).start()

                    @pl.when(foreign)
                    def _():
                        side(direction, step - 1, q, piece).start()

                    share(here, piece, q)

            late = step - LAG
            for direction in range(2):

                @pl.when((late >= 1) & (late <= lengths[direction]))
                def _():
                    piece, foreign = arrived(direction, late)

                    @pl.when(foreign)
                    def _():
                        side(direction, late - 1, q, piece).wait_recv()
                        third = 2 * chips + lax.rem(piece, 2 * half)
                        share(out.at[third, chunk(q)], third, q)

            return 0

        return lax.fori_loop(0, PARTS, each, 0)

    lax.fori_loop(0, half + SKEW * (PARTS - 1) + LAG + 1, tick, 0)

    def drain(pieces, semaphore):
        span = out.at[pl.ds(0, pieces)]
        pltpu.make_async_copy(span, span, semaphore).wait()

    keep.wait()
    drain(chips - 1, ring_sent)
    drain(half, side_sent)
    drain(chips + half, mate_sent)
    drain(chips + half, mate_recv)


def layer_kernel(
    half, tile_row, tile_col, tile_count, panels, edges, scale, weight, bias, cotangent, hidden, summed, upstream, total
):
    rows = total.shape[0]
    blk = lax.axis_index("blk")
    blks = lax.axis_size("blk")
    upper = lax.rem(blk, 2)
    live = tile_count[0]
    tiles = rows // TILE
    group_tiles = 2 * half * tiles
    total[...] = jnp.zeros_like(total)

    def multiply(b, _):
        products = []
        for i in range(BATCH):
            k = b * BATCH + i
            col = tile_col[0, k]
            position = lax.div(col, group_tiles)
            offset = lax.rem(position - blk + blks, blks)
            part = jnp.where(offset == 0, upper, jnp.where(offset == jnp.where(upper == 0, 1, blks - 1), 1 - upper, 2))
            tile = part * group_tiles + lax.rem(col, group_tiles)
            product = jnp.dot(edges[k], panels[tile], preferred_element_type=jnp.float32)
            products.append(jnp.where(k < live, product, 0.0))
        for i in range(BATCH):
            start = pl.multiple_of(tile_row[0, b * BATCH + i] * TILE, TILE)
            total[pl.ds(start, TILE), :] += products[i]
        return 0

    lax.fori_loop(0, lax.div(live + (BATCH - 1), BATCH), multiply, 0)
    for t in range(tiles):
        span = pl.ds(t * TILE, TILE)
        aggregated = (spread(scale[pl.ds(t, 1), :]) * total[span, :]).astype(jnp.bfloat16)
        summed[span, :] = aggregated
        preact = jnp.dot(aggregated, weight[...], preferred_element_type=jnp.float32) + bias[...]
        positive = preact > 0
        power = jnp.exp(jnp.minimum(preact, 0.0))
        hidden[span, :] = jnp.where(positive, preact, power - 1.0).astype(hidden.dtype)
        slope = jnp.where(positive, 1.0, power)
        upstream[span, :] = (cotangent[span, :].astype(jnp.float32) * slope).astype(upstream.dtype)


def farthest(t, size):
    step = lax.div(t + 1, 2)
    return size // 2 + jnp.where(lax.rem(t, 2) == 0, step, -step)


def sum_kernel(
    columns, half, summed, upstream, out, out_bias,
    grad, grad_bias, from_mate, bias_mate, message, inbox, line, full,
    mate_recv, bias_recv, plane_recv, line_recv, back_recv, last_recv,
    mate_sent, bias_sent, plane_sent, line_sent, back_sent, last_sent,
):
    chips = 2 * half
    blk, rep, column, upper, chip, core = place(columns, half)
    mate = (blk, rep + 1 - 2 * core)
    x, y = lax.div(column, ACROSS), lax.rem(column, ACROSS)
    deep = columns // ACROSS
    lanes = out.shape[1] // TILE

    def each_plane(act):
        def body(e, _):
            to_x = lax.rem(x + farthest(lax.div(e, ACROSS), deep), deep)
            to_y = lax.rem(y + farthest(lax.rem(e, ACROSS), ACROSS), ACROSS)
            j = to_x * ACROSS + to_y
            act((2 * j + upper, rep), j)
            return 0

        lax.fori_loop(0, columns - 1, body, 0)

    def each_line(act):
        def body(e, _):
            c = lax.rem(chip + farthest(e, chips), chips)
            act((2 * column + lax.div(c, half), 2 * lax.rem(c, half) + core))
            return 0

        lax.fori_loop(0, chips - 1, body, 0)

    barrier = pltpu.get_barrier_semaphore()
    each_line(lambda device: pl.semaphore_signal(barrier, inc=1, device_id=device, device_id_type=MESH))
    each_plane(lambda device, j: pl.semaphore_signal(barrier, inc=1, device_id=device, device_id_type=MESH))
    pl.semaphore_signal(barrier, inc=1, device_id=mate, device_id_type=MESH)

    weight_part = lax.dot_general(
        summed[...], upstream[...], (((0,), (0,)), ((), ())), preferred_element_type=jnp.float32
    )
    bias_part = jnp.sum(upstream[...].astype(jnp.float32), axis=0, keepdims=True)
    for c in range(2):
        for j in range(columns):
            r, s = divmod(c * columns + j, lanes)
            grad[c, j] = weight_part[8 * r : 8 * r + 8, TILE * s : TILE * (s + 1)]
    grad_bias[...] = jnp.zeros_like(grad_bias)
    for s in range(lanes):
        grad_bias[s : s + 1, :] = bias_part[:, TILE * s : TILE * (s + 1)]
    pl.semaphore_wait(barrier, columns + chips - 1)

    def remote(source, target, sent, received, device):
        return pltpu.make_async_remote_copy(
            src_ref=source, dst_ref=target, send_sem=sent, recv_sem=received, device_id=device, device_id_type=MESH
        )

    def landed(buffer, pieces, semaphore):
        span = buffer.at[pl.ds(0, pieces)]
        pltpu.make_async_copy(span, span, semaphore).wait()

    other = remote(grad.at[1 - core], from_mate, mate_sent, mate_recv, mate)
    other.start()
    other_bias = remote(grad_bias, bias_mate, bias_sent, bias_recv, mate)
    other_bias.start()
    other_bias.wait()
    bias_sum = grad_bias[...] + bias_mate[...]
    other.wait()
    for j in range(columns):
        message[j] = jnp.concatenate([grad[core, j] + from_mate[j], bias_sum], axis=0).astype(message.dtype)

    each_plane(lambda device, j: remote(message.at[j], inbox.at[column], plane_sent, plane_recv, device).start())
    inbox[column] = message[column]
    landed(inbox, columns - 1, plane_recv)
    line[chip] = jnp.sum(inbox[...].astype(jnp.float32), axis=0).astype(line.dtype)

    each_line(lambda device: remote(line.at[chip], line.at[chip], line_sent, line_recv, device).start())
    landed(line, chips - 1, line_recv)
    final = jnp.sum(line[...].astype(jnp.float32), axis=0)
    full[core, column] = final[0:8, :]
    out_bias[...] = final[8:16, :]

    here = full.at[core, column]
    each_plane(lambda device, j: remote(here, here, back_sent, back_recv, device).start())
    landed(full.at[core], columns - 1, back_recv)
    mine = full.at[core]
    last = remote(mine, mine, last_sent, last_recv, mate)
    last.start()
    last.wait()
    for c in range(2):
        for j in range(columns):
            r, s = divmod(c * columns + j, lanes)
            out[8 * r : 8 * r + 8, TILE * s : TILE * (s + 1)] = full[c, j]
    landed(message, columns - 1, plane_sent)
    landed(line, chips - 1, line_sent)
    landed(full.at[core], columns - 1, back_sent)


def shards(features, node_scale, weight, bias, cotangent, tile_row, tile_col, edge_weight, tile_count):
    rows, depth = features.shape
    width = weight.shape[1]
    columns = lax.axis_size("blk") // 2
    half = lax.axis_size("rep") // 2
    chips = 2 * half
    pieces = 2 * chips + 2 * half
    scale = node_scale.reshape(rows // TILE, TILE)
    vmem = pl.BlockSpec(memory_space=pltpu.VMEM)
    smem = pl.BlockSpec(memory_space=pltpu.SMEM)
    dma = pltpu.SemaphoreType.DMA

    gathered = pl.pallas_call(
        functools.partial(gather_kernel, columns, half),
        name="gather",
        out_shape=jax.ShapeDtypeStruct((pieces, rows, depth), jnp.bfloat16),
        in_specs=[vmem, vmem],
        out_specs=vmem,
        scratch_shapes=[
            pltpu.VMEM((rows, depth), jnp.bfloat16),
            dma((2 * half * PARTS,)),
            dma((2 * half * PARTS,)),
        ]
        + [dma(())] * 5,
        compiler_params=pltpu.CompilerParams(
            collective_id=0, has_side_effects=True, vmem_limit_bytes=VMEM_LIMIT
        ),
    )(features, scale)

    hidden, summed, upstream = pl.pallas_call(
        functools.partial(layer_kernel, half),
        name="layer",
        out_shape=(
            jax.ShapeDtypeStruct((rows, width), jnp.bfloat16),
            jax.ShapeDtypeStruct((rows, depth), jnp.bfloat16),
            jax.ShapeDtypeStruct((rows, width), jnp.bfloat16),
        ),
        in_specs=[smem] * 3 + [vmem] * 6,
        out_specs=(vmem, vmem, vmem),
        scratch_shapes=[pltpu.VMEM((rows, depth), jnp.float32)],
        compiler_params=pltpu.CompilerParams(vmem_limit_bytes=VMEM_LIMIT),
    )(
        tile_row, tile_col, tile_count, gathered.reshape(-1, TILE, depth), edge_weight[0], scale, weight,
        bias.reshape(1, width), cotangent,
    )

    grad_weight, bias_sum = pl.pallas_call(
        functools.partial(sum_kernel, columns, half),
        name="sum",
        out_shape=(
            jax.ShapeDtypeStruct((depth, width), jnp.float32),
            jax.ShapeDtypeStruct((8, TILE), jnp.float32),
        ),
        in_specs=[vmem, vmem],
        out_specs=(vmem, vmem),
        scratch_shapes=[
            pltpu.VMEM((2, columns, 8, TILE), jnp.float32),
            pltpu.VMEM((8, TILE), jnp.float32),
            pltpu.VMEM((columns, 8, TILE), jnp.float32),
            pltpu.VMEM((8, TILE), jnp.float32),
            pltpu.VMEM((columns, 16, TILE), WIRE),
            pltpu.VMEM((columns, 16, TILE), WIRE),
            pltpu.VMEM((chips, 16, TILE), WIRE),
            pltpu.VMEM((2, columns, 8, TILE), jnp.float32),
        ]
        + [dma(())] * 12,
        compiler_params=pltpu.CompilerParams(
            collective_id=1, has_side_effects=True, vmem_limit_bytes=VMEM_LIMIT
        ),
    )(summed, upstream)
    return hidden, grad_weight, bias_sum.reshape(-1)[:width]


def solution(mesh):
    rows = P(("blk", "rep"))
    in_specs = (
        P(("blk", "rep"), None),
        rows,
        P(),
        P(),
        P(("blk", "rep"), None),
        P(("blk", "rep"), None),
        P(("blk", "rep"), None),
        P(("blk", "rep"), None, None, None),
        rows,
    )
    out_specs = (P(("blk", "rep"), None), P(), P())
    return jax.shard_map(shards, mesh=mesh, in_specs=in_specs, out_specs=out_specs, check_vma=False)
```

time: 119 us -> 105 us (0.88)
  Pallas kernels: 115 us -> 101 us
    pallas_call x1, Pallas kernels: 76.4 us -> 60.5 us  [shards(): pl.pallas_call(functools.partial(gather_kernel, columns, half), name='gat...]
    pallas_call x1, Pallas kernels: 32.5 us -> 36.5 us  [shards(): pl.pallas_call(functools.partial(sum_kernel, columns, half), name='sum',...]
    pallas_call x1, Pallas kernels: 5.66 us -> 3.53 us  [shards(): pl.pallas_call(functools.partial(layer_kernel, half), name='layer', out_s...]
    unnamed x17 -> x19, local copies, waits for them, and re-layouts: 2.5 us -> 2.51 us
where the time goes in v2:
time: 105 us
  Pallas kernels  101 us (96%)
  local copies, waits for them, and re-layouts  3.09 us (3%)
  between operations  1.54 us (1%)
    pallas_call x1, Pallas kernels, shards(): pl.pallas_call(functools.partial(gather_kernel, columns, half), name='gat...  60.5 us
    pallas_call x1, Pallas kernels, shards(): pl.pallas_call(functools.partial(sum_kernel, columns, half), name='sum',...  36.5 us
    pallas_call x1, Pallas kernels, shards(): pl.pallas_call(functools.partial(layer_kernel, half), name='layer', out_s...  3.53 us
    unnamed x19, local copies, waits for them, and re-layouts  2.51 us

profile of v2, /device:TPU:1, one launch (start us, length us, event | category | flops | bytes accessed | tf_op | source)
XLA Modules:
  0.0 105.1 jit_solution(8232045003765651803)
XLA Ops:
  0.6 0.0 copy-start
  0.6 0.0 copy-start.1
  1.4 0.0 copy-start.2
  1.5 1.1 %copy-done.2 = bf16[1024,128]{1,0:T(8,128)(2,1)S(1)} copy-done((bf16[1024,128]{1,0:T(8,128)(2,1)S(1)}, bf16[1024,128]{1,0:T(8,128)(2,1)}, u32[]{:S(2)}) %copy-start.2) | copy-done | bytes 262168
  2.5 0.0 copy-start.4
  2.5 0.7 copy-done.4
  3.2 0.0 copy-start.3
  3.2 0.0 copy-start.5
  3.2 0.0 copy-start.6
  3.2 0.0 copy-start.7
  3.2 0.0 copy-start.8
  3.3 60.5 %gather.1 = bf16[36,1024,128]{2,1,0:T(8,128)(2,1)S(1)} custom-call(bf16[1024,128]{1,0:T(8,128)(2,1)S(1)} %copy-done.2, f32[8,128]{1,0:T(8,128)S(1)} %bitcast.8), custom_call_target="tpu_custom_call" | custom-call | tf_op jit(solution)/shard_map/gather/pallas_call | solution.py:318
  63.8 0.0 copy-done
  63.8 0.0 copy-done.1
  63.8 0.0 copy-done.3
  63.8 0.0 copy-done.5
  63.8 0.0 copy-done.6
  63.8 0.0 copy-done.7
  63.8 0.0 copy-done.8
  63.8 3.5 %layer.1 = (bf16[1024,512]{1,0:T(8,128)(2,1)}, bf16[1024,128]{1,0:T(8,128)(2,1)S(1)}, bf16[1024,512]{1,0:T(8,128)(2,1)S(1)}) custom-call(s32[1,64]{1,0:T(1,128)S(1)} %copy-done.7, s32[1,64]{1,0:T(1,128)S(1)} %copy-done.8, s32[1]{0:T(128)S(6)} %copy.13.tile_count, bf16[288,128,128]{2,1,0:T(8,128)(2,1)S(1)} %bitcast.6, bf16[64,128,128]{2,1,0:T(8,128)(2,1)S(1)} %bitcast.7, ...), custom_call_target="tpu_custom_call" | custom-call | tf_op jit(solution)/shard_map/layer/pallas_call | solution.py:335
  67.4 36.5 %sum.1 = (f32[128,512]{1,0:T(8,128)S(1)}, f32[8,128]{1,0:T(8,128)S(1)}) custom-call(bf16[1024,128]{1,0:T(8,128)(2,1)S(1)} %get-tuple-element.9.summed, bf16[1024,512]{1,0:T(8,128)(2,1)S(1)} %get-tuple-element.10.upstream), custom_call_target="tpu_custom_call" | custom-call | tf_op jit(solution)/shard_map/sum/pallas_call | solution.py:352
  103.9 0.6 slice_bitcast_fusion
  104.4 0.7 copy.14
Async XLA Ops:
  0.6 63.1 %copy-start = (bf16[1,64,128,128]{3,2,1,0:T(8,128)(2,1)S(1)}, bf16[1,64,128,128]{3,2,1,0:T(8,128)(2,1)}, u32[]{:S(2)}) copy-start(bf16[1,64,128,128]{3,2,1,0:T(8,128)(2,1)} %param.16) | copy-start | bytes 6291460
  0.6 63.1 %copy-start.1 = (bf16[1024,512]{1,0:T(8,128)(2,1)S(1)}, bf16[1024,512]{1,0:T(8,128)(2,1)}, u32[]{:S(2)}) copy-start(bf16[1024,512]{1,0:T(8,128)(2,1)} %cotangent.1) | copy-start | bytes 3145732
  1.4 1.1 %copy-start.2 = (bf16[1024,128]{1,0:T(8,128)(2,1)S(1)}, bf16[1024,128]{1,0:T(8,128)(2,1)}, u32[]{:S(2)}) copy-start(bf16[1024,128]{1,0:T(8,128)(2,1)} %features.1) | copy-start | bytes 786436
  2.5 0.7 copy-start.4
  3.2 60.6 %copy-start.3 = (bf16[128,512]{1,0:T(8,128)(2,1)S(1)}, bf16[128,512]{1,0:T(8,128)(2,1)}, u32[]{:S(2)}) copy-start(bf16[128,512]{1,0:T(8,128)(2,1)} %weight.1) | copy-start | bytes 393220
  3.2 60.6 %copy-start.5 = (f32[1024]{0:T(1024)S(1)}, f32[1024]{0:T(1024)}, u32[]{:S(2)}) copy-start(f32[1024]{0:T(1024)} %param.10) | copy-start | bytes 12292
  3.2 60.6 %copy-start.6 = (f32[512]{0:T(512)S(1)}, f32[512]{0:T(512)}, u32[]{:S(2)}) copy-start(f32[512]{0:T(512)} %param.12) | copy-start | bytes 6148
  3.2 60.6 %copy-start.7 = (s32[1,64]{1,0:T(1,128)S(1)}, s32[1,64]{1,0:T(1,128)}, u32[]{:S(2)}) copy-start(s32[1,64]{1,0:T(1,128)} %tile_row.1) | copy-start | bytes 772
  3.2 60.6 %copy-start.8 = (s32[1,64]{1,0:T(1,128)S(1)}, s32[1,64]{1,0:T(1,128)}, u32[]{:S(2)}) copy-start(s32[1,64]{1,0:T(1,128)} %tile_col.1) | copy-start | bytes 772

commit v3 on v2

--- a/solution.py
+++ b/solution.py
@@ -162,55 +162,14 @@
     drain(chips + half, mate_recv)
 
 
-def layer_kernel(
-    half, tile_row, tile_col, tile_count, panels, edges, scale, weight, bias, cotangent, hidden, summed, upstream, total
-):
-    rows = total.shape[0]
-    blk = lax.axis_index("blk")
-    blks = lax.axis_size("blk")
-    upper = lax.rem(blk, 2)
-    live = tile_count[0]
-    tiles = rows // TILE
-    group_tiles = 2 * half * tiles
-    total[...] = jnp.zeros_like(total)
-
-    def multiply(b, _):
-        products = []
-        for i in range(BATCH):
-            k = b * BATCH + i
-            col = tile_col[0, k]
-            position = lax.div(col, group_tiles)
-            offset = lax.rem(position - blk + blks, blks)
-            part = jnp.where(offset == 0, upper, jnp.where(offset == jnp.where(upper == 0, 1, blks - 1), 1 - upper, 2))
-            tile = part * group_tiles + lax.rem(col, group_tiles)
-            product = jnp.dot(edges[k], panels[tile], preferred_element_type=jnp.float32)
-            products.append(jnp.where(k < live, product, 0.0))
-        for i in range(BATCH):
-            start = pl.multiple_of(tile_row[0, b * BATCH + i] * TILE, TILE)
-            total[pl.ds(start, TILE), :] += products[i]
-        return 0
-
-    lax.fori_loop(0, lax.div(live + (BATCH - 1), BATCH), multiply, 0)
-    for t in range(tiles):
-        span = pl.ds(t * TILE, TILE)
-        aggregated = (spread(scale[pl.ds(t, 1), :]) * total[span, :]).astype(jnp.bfloat16)
-        summed[span, :] = aggregated
-        preact = jnp.dot(aggregated, weight[...], preferred_element_type=jnp.float32) + bias[...]
-        positive = preact > 0
-        power = jnp.exp(jnp.minimum(preact, 0.0))
-        hidden[span, :] = jnp.where(positive, preact, power - 1.0).astype(hidden.dtype)
-        slope = jnp.where(positive, 1.0, power)
-        upstream[span, :] = (cotangent[span, :].astype(jnp.float32) * slope).astype(upstream.dtype)
-
-
 def farthest(t, size):
     step = lax.div(t + 1, 2)
     return size // 2 + jnp.where(lax.rem(t, 2) == 0, step, -step)
 
 
-def sum_kernel(
-    columns, half, summed, upstream, out, out_bias,
-    grad, grad_bias, from_mate, bias_mate, message, inbox, line, full,
+def layer_kernel(
+    columns, half, tile_row, tile_col, tile_count, panels, edges, scale, weight, bias, cotangent,
+    hidden, out, out_bias, total, summed, upstream, grad, grad_bias, from_mate, bias_mate, message, inbox, line, full,
     mate_recv, bias_recv, plane_recv, line_recv, back_recv, last_recv,
     mate_sent, bias_sent, plane_sent, line_sent, back_sent, last_sent,
 ):
@@ -244,6 +203,40 @@
     each_plane(lambda device, j: pl.semaphore_signal(barrier, inc=1, device_id=device, device_id_type=MESH))
     pl.semaphore_signal(barrier, inc=1, device_id=mate, device_id_type=MESH)
 
+    blks = lax.axis_size("blk")
+    live = tile_count[0]
+    tiles = total.shape[0]
+    group_tiles = 2 * half * tiles
+    total[...] = jnp.zeros_like(total)
+
+    def multiply(b, _):
+        products = []
+        for i in range(BATCH):
+            k = b * BATCH + i
+            col = tile_col[0, k]
+            offset = lax.rem(lax.div(col, group_tiles) - blk + blks, blks)
+            part = jnp.where(offset == 0, upper, jnp.where(offset == jnp.where(upper == 0, 1, blks - 1), 1 - upper, 2))
+            tile = part * group_tiles + lax.rem(col, group_tiles)
+            products.append(jnp.dot(edges[k], panels[tile], preferred_element_type=jnp.float32))
+        for t in range(tiles):
+            added = total[t]
+            for i in range(BATCH):
+                k = b * BATCH + i
+                added += jnp.where((tile_row[0, k] == t) & (k < live), 1.0, 0.0) * products[i]
+            total[t] = added
+        return 0
+
+    lax.fori_loop(0, edges.shape[0] // BATCH, multiply, 0)
+    for t in range(tiles):
+        span = pl.ds(t * TILE, TILE)
+        aggregated = (spread(scale[pl.ds(t, 1), :]) * total[t]).astype(jnp.bfloat16)
+        summed[span, :] = aggregated
+        preact = jnp.dot(aggregated, weight[...], preferred_element_type=jnp.float32) + bias[...]
+        positive = preact > 0
+        power = jnp.exp(jnp.minimum(preact, 0.0))
+        hidden[span, :] = jnp.where(positive, preact, power - 1.0).astype(hidden.dtype)
+        slope = jnp.where(positive, 1.0, power)
+        upstream[span, :] = (cotangent[span, :].astype(jnp.float32) * slope).astype(upstream.dtype)
     weight_part = lax.dot_general(
         summed[...], upstream[...], (((0,), (0,)), ((), ())), preferred_element_type=jnp.float32
     )
@@ -332,33 +325,20 @@
         ),
     )(features, scale)
 
-    hidden, summed, upstream = pl.pallas_call(
-        functools.partial(layer_kernel, half),
+    hidden, grad_weight, bias_sum = pl.pallas_call(
+        functools.partial(layer_kernel, columns, half),
         name="layer",
         out_shape=(
             jax.ShapeDtypeStruct((rows, width), jnp.bfloat16),
-            jax.ShapeDtypeStruct((rows, depth), jnp.bfloat16),
-            jax.ShapeDtypeStruct((rows, width), jnp.bfloat16),
+            jax.ShapeDtypeStruct((depth, width), jnp.float32),
+            jax.ShapeDtypeStruct((8, TILE), jnp.float32),
         ),
         in_specs=[smem] * 3 + [vmem] * 6,
         out_specs=(vmem, vmem, vmem),
-        scratch_shapes=[pltpu.VMEM((rows, depth), jnp.float32)],
-        compiler_params=pltpu.CompilerParams(vmem_limit_bytes=VMEM_LIMIT),
-    )(
-        tile_row, tile_col, tile_count, gathered.reshape(-1, TILE, depth), edge_weight[0], scale, weight,
-        bias.reshape(1, width), cotangent,
-    )
-
-    grad_weight, bias_sum = pl.pallas_call(
-        functools.partial(sum_kernel, columns, half),
-        name="sum",
-        out_shape=(
-            jax.ShapeDtypeStruct((depth, width), jnp.float32),
-            jax.ShapeDtypeStruct((8, TILE), jnp.float32),
-        ),
-        in_specs=[vmem, vmem],
-        out_specs=(vmem, vmem),
         scratch_shapes=[
+            pltpu.VMEM((rows // TILE, TILE, depth), jnp.float32),
+            pltpu.VMEM((rows, depth), jnp.bfloat16),
+            pltpu.VMEM((rows, width), jnp.bfloat16),
             pltpu.VMEM((2, columns, 8, TILE), jnp.float32),
             pltpu.VMEM((8, TILE), jnp.float32),
             pltpu.VMEM((columns, 8, TILE), jnp.float32),
@@ -372,7 +352,10 @@
         compiler_params=pltpu.CompilerParams(
             collective_id=1, has_side_effects=True, vmem_limit_bytes=VMEM_LIMIT
         ),
-    )(summed, upstream)
+    )(
+        tile_row, tile_col, tile_count, gathered.reshape(-1, TILE, depth), edge_weight[0], scale, weight,
+        bias.reshape(1, width), cotangent,
+    )
     return hidden, grad_weight, bias_sum.reshape(-1)[:width]
 
 

time: 105 us -> 103 us (0.981)
  Pallas kernels: 101 us -> 97.5 us
    pallas_call x2 -> x1, Pallas kernels: 40 us -> 37 us  [shards(): pl.pallas_call(functools.partial(layer_kernel, columns, half), name='laye...]
    unnamed x19 -> x20, local copies, waits for them, and re-layouts: 2.51 us -> 3.47 us
where the time goes in v3:
time: 103 us
  Pallas kernels  97.5 us (95%)
  local copies, waits for them, and re-layouts  4.06 us (4%)
  between operations  1.54 us (1%)
    pallas_call x1, Pallas kernels, shards(): pl.pallas_call(functools.partial(gather_kernel, columns, half), name='gat...  60.5 us
    pallas_call x1, Pallas kernels, shards(): pl.pallas_call(functools.partial(layer_kernel, columns, half), name='laye...  37 us
    unnamed x20, local copies, waits for them, and re-layouts  3.47 us

profile of v3, /device:TPU:1, one launch (start us, length us, event | category | flops | bytes accessed | tf_op | source)
XLA Modules:
  0.0 103.1 jit_solution(11397463757560104425)
XLA Ops:
  0.6 0.0 copy-start
  0.6 0.0 copy-start.1
  1.4 0.0 copy-start.2
  1.5 1.1 %copy-done.2 = bf16[1024,128]{1,0:T(8,128)(2,1)S(1)} copy-done((bf16[1024,128]{1,0:T(8,128)(2,1)S(1)}, bf16[1024,128]{1,0:T(8,128)(2,1)}, u32[]{:S(2)}) %copy-start.2) | copy-done | bytes 262168
  2.5 0.0 copy-start.4
  2.5 0.7 copy-done.4
  3.2 0.0 copy-start.3
  3.2 0.0 copy-start.5
  3.2 0.0 copy-start.6
  3.2 0.0 copy-start.7
  3.2 0.0 copy-start.8
  3.3 60.5 %gather.1 = bf16[36,1024,128]{2,1,0:T(8,128)(2,1)S(1)} custom-call(bf16[1024,128]{1,0:T(8,128)(2,1)S(1)} %copy-done.2, f32[8,128]{1,0:T(8,128)S(1)} %bitcast.8), custom_call_target="tpu_custom_call" | custom-call | tf_op jit(solution)/shard_map/gather/pallas_call | solution.py:311
  63.8 0.0 copy-done
  63.8 0.0 copy-done.1
  63.8 0.0 copy-done.3
  63.8 0.0 copy-done.5
  63.8 0.0 copy-done.6
  63.8 0.0 copy-done.7
  63.8 0.0 copy-done.8
  63.8 37.0 %layer.1 = (bf16[1024,512]{1,0:T(8,128)(2,1)S(1)}, f32[128,512]{1,0:T(8,128)S(1)}, f32[8,128]{1,0:T(8,128)S(1)}) custom-call(s32[1,64]{1,0:T(1,128)S(1)} %copy-done.7, s32[1,64]{1,0:T(1,128)S(1)} %copy-done.8, s32[1]{0:T(128)S(6)} %copy.14.tile_count, bf16[288,128,128]{2,1,0:T(8,128)(2,1)S(1)} %bitcast.6, bf16[64,128,128]{2,1,0:T(8,128)(2,1)S(1)} %bitcast.7, ...), custom_call_target="tpu_custom_call" | custom-call | tf_op jit(solution)/shard_map/layer/pallas_call | solution.py:328
  100.9 0.6 slice_bitcast_fusion
  101.4 1.0 copy.15
  102.4 0.7 copy.16
Async XLA Ops:
  0.6 63.1 %copy-start = (bf16[1,64,128,128]{3,2,1,0:T(8,128)(2,1)S(1)}, bf16[1,64,128,128]{3,2,1,0:T(8,128)(2,1)}, u32[]{:S(2)}) copy-start(bf16[1,64,128,128]{3,2,1,0:T(8,128)(2,1)} %param.16) | copy-start | bytes 6291460
  0.6 63.1 %copy-start.1 = (bf16[1024,512]{1,0:T(8,128)(2,1)S(1)}, bf16[1024,512]{1,0:T(8,128)(2,1)}, u32[]{:S(2)}) copy-start(bf16[1024,512]{1,0:T(8,128)(2,1)} %cotangent.1) | copy-start | bytes 3145732
  1.4 1.1 %copy-start.2 = (bf16[1024,128]{1,0:T(8,128)(2,1)S(1)}, bf16[1024,128]{1,0:T(8,128)(2,1)}, u32[]{:S(2)}) copy-start(bf16[1024,128]{1,0:T(8,128)(2,1)} %features.1) | copy-start | bytes 786436
  2.5 0.7 copy-start.4
  3.2 60.6 %copy-start.3 = (bf16[128,512]{1,0:T(8,128)(2,1)S(1)}, bf16[128,512]{1,0:T(8,128)(2,1)}, u32[]{:S(2)}) copy-start(bf16[128,512]{1,0:T(8,128)(2,1)} %weight.1) | copy-start | bytes 393220
  3.2 60.6 %copy-start.5 = (f32[1024]{0:T(1024)S(1)}, f32[1024]{0:T(1024)}, u32[]{:S(2)}) copy-start(f32[1024]{0:T(1024)} %param.10) | copy-start | bytes 12292
  3.2 60.6 %copy-start.6 = (f32[512]{0:T(512)S(1)}, f32[512]{0:T(512)}, u32[]{:S(2)}) copy-start(f32[512]{0:T(512)} %param.12) | copy-start | bytes 6148
  3.2 60.6 %copy-start.7 = (s32[1,64]{1,0:T(1,128)S(1)}, s32[1,64]{1,0:T(1,128)}, u32[]{:S(2)}) copy-start(s32[1,64]{1,0:T(1,128)} %tile_row.1) | copy-start | bytes 772
  3.2 60.6 %copy-start.8 = (s32[1,64]{1,0:T(1,128)S(1)}, s32[1,64]{1,0:T(1,128)}, u32[]{:S(2)}) copy-start(s32[1,64]{1,0:T(1,128)} %tile_col.1) | copy-start | bytes 772
